TPU v7x, 128 devices: a whole 4x4x4 slice. The times are simulated.
128 devices in a mesh: dp: 4 (over y), expert: 32 (over z, x, core).
Axes of the slice: x: 4, y: 4, z: 4, core: 2. Of those that a mesh axis runs over, the one named last changes fastest.
Arguments:
- inputs: bfloat16 [2, 32, 256, 768], P(None, 'expert', 'dp'), may hold values from -6 to 6
- wqkv: bfloat16 [768, 2304], P(('dp', 'expert')), may hold values from -0.21875 to 0.21875
- wo: bfloat16 [768, 768], P(('dp', 'expert')), may hold values from -0.625 to 0.625
- wr: bfloat16 [768, 64], P(('dp', 'expert')), may hold values from -0.15625 to 0.15625
- gain_one: bfloat16 [768], P(('dp', 'expert')), may hold values from 0.099609375 to 1.8984375
- gain_two: bfloat16 [768], P(('dp', 'expert')), may hold values from 0.099609375 to 1.8984375
- rel_bias: bfloat16 [384], P(('dp', 'expert')), may hold values from -4 to 4
- w_in: bfloat16 [64, 768, 3072], P('expert', None, 'dp'), may hold values from -0.21875 to 0.21875
- w_out: bfloat16 [64, 3072, 768], P('expert', 'dp'), may hold values from -0.109375 to 0.109375
- routes: int32 [2, 32, 256, 2], P(None, 'expert', 'dp'), may hold values from 0 to 63, all different within a row; in each aligned block of 64 rows (0 to 63, 64 to 127, ..., all dimensions but the last counted through in order) at most 3 rows name the same one
- lengths: int32 [2, 32, 3], P(None, 'expert'), may hold values from 1 to 224, 256 in all within a row
- cotangent: bfloat16 [2, 32, 256, 768], P(None, 'expert', 'dp'), may hold values from -6 to 6
Outputs:
- output: bfloat16 [2, 32, 256, 768], P(None, 'expert', 'dp')
- input_grad: float32 [2, 32, 256, 768], P(None, 'expert', 'dp')
- wqkv_grad: float32 [768, 2304], P(('dp', 'expert'))
- wo_grad: float32 [768, 768], P(('dp', 'expert'))
- wr_grad: float32 [768, 64], P(('dp', 'expert'))
- gain_one_grad: float32 [768], P(('dp', 'expert'))
- gain_two_grad: float32 [768], P(('dp', 'expert'))
- rel_bias_grad: float32 [384], P(('dp', 'expert'))
- w_in_grad: float32 [64, 768, 3072], P('expert', None, 'dp')
- w_out_grad: float32 [64, 3072, 768], P('expert', 'dp')
Inputs may be any that keep to these rules, and one draw needn't show every extreme that they name: `routes`: each token names two different experts; in the 64 rows of one device in one micro-batch no expert is named more than 3 times, a bound that some block reaches. The 3 lengths of a pack add up to 256.
All inputs are finite; a program needn't handle non-finite values.
Results may differ from a plain program's by a relative error of at most 0.018.
Values may be sent and summed in bfloat16 or wider, within the bound.
No kernel may reach another device: no remote copies, remote signals or barrier semaphores. Data moves between devices by JAX's collectives and lax.ppermute only.
A program may use at most 192 MiB of HBM per device.

v0:
```python
import math

import jax
import jax.numpy as jnp
from jax import lax
from jax.sharding import PartitionSpec as P

HEADS = 12
HEAD_DIM = 64
BUCKETS = 32
CAP = 3


exact_mode = lax.Precision.HIGHEST


def rms_scale(values):
    return lax.rsqrt(jnp.mean(values * values, axis=-1, keepdims=True) + 1e-06)


def softmax_last(scores):
    peak = jnp.max(scores, axis=-1, keepdims=True)
    weights = jnp.exp(scores - peak)
    return weights / jnp.sum(weights, axis=-1, keepdims=True)


def norm_backward(grad_normed, values, scale, gain):
    grad_scaled = grad_normed * gain
    inner = jnp.mean(grad_scaled * values, axis=-1, keepdims=True)
    grad_values = scale * grad_scaled - values * scale * scale * scale * inner
    return (grad_values, jnp.sum(grad_normed * values * scale, axis=0))


def bucket_index(query_places, key_places, far_step):
    gap = jnp.maximum(query_places[:, None] - key_places[None, :], 0)
    halfway = BUCKETS // 2
    farther = jnp.minimum(BUCKETS - 1, halfway + (gap - halfway) // far_step)
    return jnp.where(gap < halfway, gap, farther)


def segment_of(lengths_row, places):
    bounds = jnp.cumsum(lengths_row)[:-1]
    return jnp.sum((places[:, None] >= bounds[None, :]).astype(jnp.int32), axis=1)


def slot_numbers(routes_flat, experts_all):
    marks = (routes_flat[:, None] == jnp.arange(experts_all, dtype=jnp.int32)[None, :]).astype(
        jnp.int32
    )
    before = jnp.cumsum(marks, axis=0) - marks
    return jnp.sum(marks * before, axis=1)


def body(
    inputs, wqkv, wo, wr, gain_one, gain_two, rel_bias, w_in, w_out, routes, lengths, cotangent
):
    micro_total = inputs.shape[0]
    tokens_here = inputs.shape[2]
    width = inputs.shape[3]
    groups = lax.axis_size("dp")
    position = lax.axis_index("dp")
    owners = lax.axis_size("expert")
    local_experts = w_in.shape[0]
    experts_all = local_experts * owners
    span = tokens_here * groups
    far_step = max(1, (span - tokens_here // 2 - 1 - BUCKETS // 2) // BUCKETS)
    score_scale = 1.0 / math.sqrt(HEAD_DIM)
    query_places = position * tokens_here + jnp.arange(tokens_here, dtype=jnp.int32)
    key_places = jnp.arange(span, dtype=jnp.int32)
    buckets = bucket_index(query_places, key_places, far_step)
    table_marks = (buckets[:, :, None] == jnp.arange(BUCKETS, dtype=jnp.int32)).astype(jnp.float32)
    expert_ids = jnp.arange(experts_all, dtype=jnp.int32)
    grad_wqkv = jnp.zeros((width, 3 * width), jnp.float32)
    grad_wo = jnp.zeros((width, width), jnp.float32)
    grad_wr = jnp.zeros((width, experts_all), jnp.float32)
    grad_gain_one = jnp.zeros((width,), jnp.float32)
    grad_gain_two = jnp.zeros((width,), jnp.float32)
    grad_table = jnp.zeros((HEADS, BUCKETS), jnp.float32)
    grad_in = jnp.zeros((local_experts, width, w_in.shape[2] * groups), jnp.float32)
    grad_out = jnp.zeros((local_experts, w_out.shape[1] * groups, width), jnp.float32)
    outputs = []
    input_grads = []
    for micro_index in range(micro_total):
        gathered = (
            lax.all_gather(wqkv, ("dp", "expert"), axis=0, tiled=True),
            lax.all_gather(wo, ("dp", "expert"), axis=0, tiled=True),
            lax.all_gather(wr, ("dp", "expert"), axis=0, tiled=True),
            lax.all_gather(gain_one, ("dp", "expert"), axis=0, tiled=True),
            lax.all_gather(gain_two, ("dp", "expert"), axis=0, tiled=True),
            lax.all_gather(rel_bias, ("dp", "expert"), axis=0, tiled=True),
        )
        full_qkv = gathered[0]
        full_out = gathered[1]
        full_router = gathered[2]
        first_gain = gathered[3].astype(jnp.float32)
        second_gain = gathered[4].astype(jnp.float32)
        table = gathered[5].astype(jnp.float32).reshape(HEADS, BUCKETS)
        values = inputs[micro_index, 0].astype(jnp.float32)
        first_scale = rms_scale(values)
        normed = (values * first_scale * first_gain).astype(jnp.bfloat16)
        qkv = jnp.dot(normed, full_qkv, preferred_element_type=jnp.float32).astype(jnp.bfloat16)
        queries = qkv[:, :width]
        key_rows, value_rows = (
            lax.all_gather(qkv[:, width : 2 * width], "dp", axis=0, tiled=True),
            lax.all_gather(qkv[:, 2 * width :], "dp", axis=0, tiled=True),
        )
        key_segment = segment_of(lengths[micro_index, 0], key_places)
        query_segment = segment_of(lengths[micro_index, 0], query_places)
        allowed = (query_segment[:, None] == key_segment[None, :]) & (
            query_places[:, None] >= key_places[None, :]
        )
        bias = jnp.einsum("qkb,hb->hqk", table_marks, table, precision=exact_mode)
        query_heads = queries.reshape(tokens_here, HEADS, HEAD_DIM)
        key_heads = key_rows.reshape(span, HEADS, HEAD_DIM)
        value_heads = value_rows.reshape(span, HEADS, HEAD_DIM)
        raw = jnp.einsum("qhd,khd->hqk", query_heads, key_heads, preferred_element_type=jnp.float32)
        scores = jnp.where(allowed[None], raw * score_scale + bias, -1000000000.0)
        probs = softmax_last(scores)
        probs_low = probs.astype(jnp.bfloat16)
        mixed = jnp.einsum(
            "hqk,khd->qhd", probs_low, value_heads, preferred_element_type=jnp.float32
        )
        mixed = mixed.reshape(tokens_here, width).astype(jnp.bfloat16)
        middle = values + jnp.dot(mixed, full_out, preferred_element_type=jnp.float32)
        second_scale = rms_scale(middle)
        entering = (middle * second_scale * second_gain).astype(jnp.bfloat16)
        logits = jnp.dot(entering, full_router, preferred_element_type=jnp.float32)
        route_rows = routes[micro_index, 0]
        picked = (route_rows[:, :, None] == expert_ids).astype(jnp.float32)
        chosen = jnp.einsum("tke,te->tk", picked, logits, precision=exact_mode)
        gates = softmax_last(chosen)
        routes_flat = route_rows.reshape(-1)
        target = routes_flat * CAP + slot_numbers(routes_flat, experts_all)
        copies = jnp.repeat(entering, 2, axis=0)
        sending = jnp.zeros((experts_all * CAP, width), jnp.bfloat16).at[target].set(copies)
        arrived = lax.all_to_all(
            sending.reshape(experts_all, CAP, width),
            "expert",
            split_axis=0,
            concat_axis=1,
            tiled=True,
        )
        first_full, second_full = (
            lax.all_gather(w_in, "dp", axis=2, tiled=True),
            lax.all_gather(w_out, "dp", axis=1, tiled=True),
        )
        raised = jnp.einsum("erd,edf->erf", arrived, first_full, preferred_element_type=jnp.float32)
        active = jax.nn.gelu(raised).astype(jnp.bfloat16)
        result = jnp.einsum("erf,efd->erd", active, second_full, preferred_element_type=jnp.float32)
        result = result.astype(jnp.bfloat16)
        returned = lax.all_to_all(result, "expert", split_axis=1, concat_axis=0, tiled=True)
        picked_rows = returned.reshape(experts_all * CAP, width)[target].reshape(
            tokens_here, 2, width
        )
        picked_rows = picked_rows.astype(jnp.float32)
        mixture = jnp.einsum("tk,tkd->td", gates, picked_rows, precision=exact_mode)
        outputs.append((middle + mixture).astype(jnp.bfloat16))
        grad_top = cotangent[micro_index, 0].astype(jnp.float32)
        grad_gates = jnp.einsum("tkd,td->tk", picked_rows, grad_top, precision=exact_mode)
        grad_rows = (gates[:, :, None] * grad_top[:, None, :]).astype(jnp.bfloat16)
        grad_chosen = gates * (grad_gates - jnp.sum(gates * grad_gates, axis=-1, keepdims=True))
        grad_logits = jnp.einsum("tk,tke->te", grad_chosen, picked, precision=exact_mode).astype(
            jnp.bfloat16
        )
        grad_sending = (
            jnp.zeros((experts_all * CAP, width), jnp.bfloat16)
            .at[target]
            .set(grad_rows.reshape(-1, width))
        )
        grad_result = lax.all_to_all(
            grad_sending.reshape(experts_all, CAP, width),
            "expert",
            split_axis=0,
            concat_axis=1,
            tiled=True,
        )
        gelu_value, gelu_pull = jax.vjp(jax.nn.gelu, raised)
        grad_active = jnp.einsum(
            "erd,efd->erf", grad_result, second_full, preferred_element_type=jnp.float32
        )
        grad_raised = gelu_pull(grad_active)[0].astype(jnp.bfloat16)
        grad_out = grad_out + jnp.einsum(
            "erf,erd->efd", active, grad_result, preferred_element_type=jnp.float32
        )
        grad_in = grad_in + jnp.einsum(
            "erd,erf->edf", arrived, grad_raised, preferred_element_type=jnp.float32
        )
        grad_arrived = jnp.einsum(
            "erf,edf->erd", grad_raised, first_full, preferred_element_type=jnp.float32
        )
        grad_back = lax.all_to_all(
            grad_arrived.astype(jnp.bfloat16), "expert", split_axis=1, concat_axis=0, tiled=True
        ).astype(grad_arrived.dtype)
        grad_copies = grad_back.reshape(experts_all * CAP, width)[target].reshape(
            tokens_here, 2, width
        )
        grad_entering = jnp.sum(grad_copies, axis=1) + jnp.einsum(
            "te,de->td", grad_logits, full_router, preferred_element_type=jnp.float32
        )
        grad_wr = grad_wr + jnp.einsum(
            "td,te->de", entering, grad_logits, preferred_element_type=jnp.float32
        )
        grad_middle_norm, gain_two_part = norm_backward(
            grad_entering, middle, second_scale, second_gain
        )
        grad_gain_two = grad_gain_two + gain_two_part
        grad_middle = grad_top + grad_middle_norm
        grad_branch = grad_middle.astype(jnp.bfloat16)
        grad_wo = grad_wo + jnp.einsum(
            "td,te->de", mixed, grad_branch, preferred_element_type=jnp.float32
        )
        grad_mixed = jnp.einsum(
            "te,de->td", grad_branch, full_out, preferred_element_type=jnp.float32
        )
        grad_mixed_heads = grad_mixed.astype(jnp.bfloat16).reshape(tokens_here, HEADS, HEAD_DIM)
        grad_probs = jnp.einsum(
            "qhd,khd->hqk", grad_mixed_heads, value_heads, preferred_element_type=jnp.float32
        )
        grad_value_heads = jnp.einsum(
            "hqk,qhd->khd", probs_low, grad_mixed_heads, preferred_element_type=jnp.float32
        )
        grad_scores = probs * (grad_probs - jnp.sum(probs * grad_probs, axis=-1, keepdims=True))
        grad_table = grad_table + jnp.einsum(
            "hqk,qkb->hb", grad_scores, table_marks, precision=exact_mode
        )
        grad_raw = (grad_scores * score_scale).astype(jnp.bfloat16)
        grad_queries = jnp.einsum(
            "hqk,khd->qhd", grad_raw, key_heads, preferred_element_type=jnp.float32
        )
        grad_key_heads = jnp.einsum(
            "hqk,qhd->khd", grad_raw, query_heads, preferred_element_type=jnp.float32
        )
        grad_keys, grad_values = (
            lax.psum_scatter(
                grad_key_heads.reshape(span, width).astype(jnp.bfloat16),
                "dp",
                scatter_dimension=0,
                tiled=True,
            ).astype(jnp.float32),
            lax.psum_scatter(
                grad_value_heads.reshape(span, width).astype(jnp.bfloat16),
                "dp",
                scatter_dimension=0,
                tiled=True,
            ).astype(jnp.float32),
        )
        grad_qkv = jnp.concatenate(
            [grad_queries.reshape(tokens_here, width), grad_keys, grad_values], axis=1
        )
        grad_qkv = grad_qkv.astype(jnp.bfloat16)
        grad_wqkv = grad_wqkv + jnp.einsum(
            "td,te->de", normed, grad_qkv, preferred_element_type=jnp.float32
        )
        grad_normed = jnp.einsum(
            "te,de->td", grad_qkv, full_qkv, preferred_element_type=jnp.float32
        )
        grad_values_in, gain_one_part = norm_backward(grad_normed, values, first_scale, first_gain)
        grad_gain_one = grad_gain_one + gain_one_part
        input_grads.append(grad_middle + grad_values_in)
    shards = (
        lax.psum_scatter(grad_wqkv, ("dp", "expert"), scatter_dimension=0, tiled=True),
        lax.psum_scatter(grad_wo, ("dp", "expert"), scatter_dimension=0, tiled=True),
        lax.psum_scatter(grad_wr, ("dp", "expert"), scatter_dimension=0, tiled=True),
        lax.psum_scatter(grad_gain_one, ("dp", "expert"), scatter_dimension=0, tiled=True),
        lax.psum_scatter(grad_gain_two, ("dp", "expert"), scatter_dimension=0, tiled=True),
        lax.psum_scatter(grad_table.reshape(-1), ("dp", "expert"), scatter_dimension=0, tiled=True),
    )
    expert_in_grad, expert_out_grad = (
        lax.psum_scatter(
            grad_in.astype(jnp.bfloat16), "dp", scatter_dimension=2, tiled=True
        ).astype(jnp.float32),
        lax.psum_scatter(
            grad_out.astype(jnp.bfloat16), "dp", scatter_dimension=1, tiled=True
        ).astype(jnp.float32),
    )
    output = jnp.stack(outputs)[:, None]
    input_grad = jnp.stack(input_grads)[:, None]
    return (
        output,
        input_grad,
        shards[0],
        shards[1],
        shards[2],
        shards[3],
        shards[4],
        shards[5],
        expert_in_grad,
        expert_out_grad,
    )


def solution(mesh):
    in_specs = (
        P(None, "expert", "dp", None),
        P(("dp", "expert"), None),
        P(("dp", "expert"), None),
        P(("dp", "expert"), None),
        P(("dp", "expert")),
        P(("dp", "expert")),
        P(("dp", "expert")),
        P("expert", None, "dp"),
        P("expert", "dp", None),
        P(None, "expert", "dp", None),
        P(None, "expert", None),
        P(None, "expert", "dp", None),
    )
    out_specs = (
        P(None, "expert", "dp", None),
        P(None, "expert", "dp", None),
        P(("dp", "expert"), None),
        P(("dp", "expert"), None),
        P(("dp", "expert"), None),
        P(("dp", "expert")),
        P(("dp", "expert")),
        P(("dp", "expert")),
        P("expert", None, "dp"),
        P("expert", "dp", None),
    )
    return jax.shard_map(body, mesh=mesh, in_specs=in_specs, out_specs=out_specs, check_vma=False)
```

profile of v0, /device:TPU:0, one launch (start us, length us, event | category | flops | bytes accessed | tf_op | source)
XLA Modules:
  0.0 1307.2 jit_solution(10075187384616892072)
XLA Ops:
  11.1 68.4 %all-reduce.12 = (bf16[768]{0:T(1024)(128)(2,1)S(1)}, bf16[384]{0:T(512)(128)(2,1)S(1)}, bf16[768]{0:T(1024)(128)(2,1)S(1)}) all-reduce(bf16[768]{0:T(1024)(128)(2,1)S(1)} %dynamic-update-slice, bf16[384]{0:T(512)(128)(2,1)S(1)} %dynamic-update-slice.1, ...), channel_id=1, replica_groups=mesh['dp'=4,'expert'=32] {'dp','expert'}, use_global_device_ids=true, to_apply=%add | all-reduce | flops 1920 | bytes 7680
  82.6 33.3 %all-gather.2 = bf16[128,6,64]{2,1,0:T(8,128)(2,1)S(1)} all-gather(bf16[1,6,64]{2,1,0:T(8,128)(2,1)S(1)} %bitcast.339), channel_id=1, replica_groups=mesh['dp'=4,'expert'=32] {'dp','expert'}, dimensions={0}, use_global_device_ids=true | all-gather | bytes 99072 | tf_op jit(solution)/shard_map/all_gather | solution.py:87
  128.3 16.9 %all-gather.12.cloned.1.call-done = bf16[128,6,2304]{2,1,0:T(8,128)(2,1)} async-done(((bf16[1,6,2304]{2,1,0:T(8,128)(2,1)}), bf16[128,6,2304]{2,1,0:T(8,128)(2,1)}) %all-gather.12.cloned.1.call-update) | async-done | bytes 3538960 | tf_op jit(solution)/shard_map/all_gather | solution.py:85
  154.6 14.8 %all_gather.55 = bf16[256,768]{1,0:T(8,128)(2,1)} all-gather(bf16[64,768]{1,0:T(8,128)(2,1)} %get-tuple-element.81), channel_id=1, replica_groups=mesh['dp'=4,'expert'=32] {'dp'}, dimensions={0}, use_global_device_ids=true | all-gather | bytes 491520 | tf_op jit(solution)/shard_map/all_gather | solution.py:104
  173.2 14.6 %all_gather.47 = bf16[256,768]{1,0:T(8,128)(2,1)S(1)} all-gather(bf16[64,768]{1,0:T(8,128)(2,1)S(1)} %get-tuple-element.78), channel_id=1, replica_groups=mesh['dp'=4,'expert'=32] {'dp'}, dimensions={0}, use_global_device_ids=true | all-gather | bytes 491520 | tf_op jit(solution)/shard_map/all_gather | solution.py:104
  188.1 14.1 %all_gather.46 = bf16[256,768]{1,0:T(8,128)(2,1)S(1)} all-gather(bf16[64,768]{1,0:T(8,128)(2,1)S(1)} %get-tuple-element.80), channel_id=1, replica_groups=mesh['dp'=4,'expert'=32] {'dp'}, dimensions={0}, use_global_device_ids=true | all-gather | bytes 491520 | tf_op jit(solution)/shard_map/all_gather | solution.py:105
  221.4 14.3 %all_gather.54 = bf16[256,768]{1,0:T(8,128)(2,1)S(1)} all-gather(bf16[64,768]{1,0:T(8,128)(2,1)S(1)} %copy-done.63), channel_id=1, replica_groups=mesh['dp'=4,'expert'=32] {'dp'}, dimensions={0}, use_global_device_ids=true | all-gather | bytes 491520 | tf_op jit(solution)/shard_map/all_gather | solution.py:105
  239.6 8.8 all-gather.8.cloned.1.call-done
  248.4 6.8 fusion.53
  255.1 86.6 %all-gather.10.cloned.1.call-done = bf16[2,3072,768]{2,1,0:T(8,128)(2,1)} async-done(((bf16[2,768,768]{2,1,0:T(8,128)(2,1)}), bf16[2,3072,768]{2,1,0:T(8,128)(2,1)}) %all-gather.10.cloned.1.call-update) | async-done | bytes 9437200 | tf_op jit(solution)/shard_map/all_gather | solution.py:145
  341.7 6.2 convolution_convert_fusion.9
  349.0 7.2 all-to-all-start.1
  377.2 8.3 all-to-all-done.4
  387.5 7.7 fusion.10
  403.7 8.7 all-to-all-done.5
  426.7 8.7 all-to-all-done.2
  441.1 6.4 convolution_convert_fusion.8
  453.3 8.5 all-to-all-done.3
  476.4 7.7 all-to-all-done.6
  485.4 7.7 fusion.17
  533.3 10.9 fusion.42
  545.2 11.0 add_convert_fusion
  557.5 7.8 fusion.51
  565.3 10.4 add_convert_fusion.1
  587.9 22.7 %reduce-scatter.27.cloned.1.call-done = bf16[64,768]{1,0:T(8,128)(2,1)} async-done(((bf16[256,768]{1,0:T(8,128)(2,1)}), bf16[64,768]{1,0:T(8,128)(2,1)}) %reduce-scatter.27.cloned.1.call-update) | async-done | bytes 98320
  617.2 370.5 %fusion.152 = (f32[8,2304]{1,0:T(8,128)}, f32[8,768]{1,0:T(8,128)}) fusion(f32[768,2304]{1,0:T(8,128)} %convolution_add_fusion, f32[768,768]{1,0:T(8,128)} %convolution_add_fusion.1), kind=kCustom, calls=%all-reduce-scatter.2 | all-reduce-scatter fusion | flops 3145729 | bytes 9535488
  1005.6 12.9 collective-permute-start.54
  1122.2 6.0 collective-permute-start.15
  1132.2 6.5 collective-permute-start.11
  1140.3 65.0 %all-reduce.11 = (f32[768]{0:T(1024)S(1)}, f32[768]{0:T(1024)S(1)}, f32[384]{0:T(512)S(1)}) all-reduce(f32[768]{0:T(1024)S(1)} %add.237, f32[768]{0:T(1024)S(1)} %add.238, f32[384]{0:T(512)S(1)} %copy-done.134), channel_id=9, replica_groups=mesh['dp'=4,'expert'=32] {'dp','expert'}, use_global_device_ids=true, to_apply=%region_45.46.clone | all-reduce | flops 1920 | bytes 15360
  1225.3 27.9 %concatenate.11 = f32[262,768]{1,0:T(8,128)S(1)} concatenate(f32[6,768]{1,0:T(8,128)} %copy-done.113, f32[8,768]{1,0:T(8,128)} %collective-permute-done.62, f32[8,768]{1,0:T(8,128)} %collective-permute-done.61, f32[8,768]{1,0:T(8,128)} %collective-permute-done.60, f32[8,768]{1,0:T(8,128)} %collective-permute-done.59, f32[8,768]{1,0:T(8,128)} %collective-permute-done.58, ...), dimensions={0} | concatenate | bytes 1609728
  1270.9 20.3 %concatenate.10 = f32[262,2304]{1,0:T(8,128)S(1)} concatenate(f32[6,2304]{1,0:T(8,128)S(1)} %copy-done.79, f32[8,2304]{1,0:T(8,128)S(1)} %copy-done.77, f32[8,2304]{1,0:T(8,128)S(1)} %copy-done.81, f32[8,2304]{1,0:T(8,128)S(1)} %copy-done.83, f32[8,2304]{1,0:T(8,128)S(1)} %copy-done.85, f32[8,2304]{1,0:T(8,128)S(1)} %copy-done.87, f32[8,2304]{1,0:T(8,128)S(1)} %copy-done.89, ...), dimensions={0} | concatenate | bytes 4829184
  (666 shorter events, 362.1 us)
Async XLA Ops:
  7.2 118.0 %all-gather.14.cloned.1.call-start = ((), (), s32[]{:S(2)}) async-start(), calls=%async_computation.19 | async-start | bytes 1585152 | tf_op jit(solution)/shard_map/all_gather | solution.py:86
  7.9 137.3 %all-gather.12.cloned.1.call-start = ((), (), s32[]{:S(2)}) async-start(), calls=%async_computation.18 | async-start | bytes 4755456 | tf_op jit(solution)/shard_map/all_gather | solution.py:85
  8.7 239.6 %all-gather.8.cloned.1.call-start = ((), (), s32[]{:S(2)}) async-start(), calls=%async_computation.14 | async-start | bytes 11796480 | tf_op jit(solution)/shard_map/all_gather | solution.py:144
  9.5 332.3 %all-gather.10.cloned.1.call-start = ((), (), s32[]{:S(2)}) async-start(), calls=%async_computation.15 | async-start | bytes 11796480 | tf_op jit(solution)/shard_map/all_gather | solution.py:145
  213.6 24.7 %all-to-all-start = ((bf16[64,3,768]{2,1,0:T(4,128)(2,1)}), bf16[64,3,768]{2,1,0:T(4,128)(2,1)}, u32[]{:S(2)}, u32[]{:S(2)}) async-start(bf16[64,3,768]{2,1,0:T(4,128)(2,1)} %reshape.419), calls=%async_computation | async-start | bytes 786432 | tf_op jit(solution)/shard_map/all_to_all | solution.py:136
  501.1 79.2 %reduce-scatter.29.cloned.1.call-start = ((), (), s32[]{:S(2)}) async-start(), calls=%async_computation.23 | async-start | bytes 491520
  522.3 59.0 %reduce-scatter.25.cloned.1.call-start = ((), (), s32[]{:S(2)}) async-start(), calls=%async_computation.21 | async-start | bytes 491520
  527.9 58.9 %reduce-scatter.23.cloned.1.call-start = ((), (), s32[]{:S(2)}) async-start(), calls=%async_computation.20 | async-start | bytes 491520
  531.0 79.7 %reduce-scatter.27.cloned.1.call-start = ((), (), s32[]{:S(2)}) async-start(), calls=%async_computation.22 | async-start | bytes 491520
  533.2 493.9 %all-reduce.16.cloned.1.call-start = ((), (), s32[]{:S(2)}) async-start(), calls=%async_computation.24 | async-start | bytes 786432
  545.2 746.6 %reduce-scatter.21.cloned.1.call-start = ((), (), s32[]{:S(2)}) async-start(), calls=%async_computation.17 | async-start | bytes 11796480 | tf_op jit(solution)/shard_map/reduce_scatter | solution.py:272
  556.3 739.8 %reduce-scatter.19.cloned.1.call-start = ((), (), s32[]{:S(2)}) async-start(), calls=%async_computation.16 | async-start | bytes 11796480 | tf_op jit(solution)/shard_map/reduce_scatter | solution.py:269
  998.0 20.5 %collective-permute-start.58 = (f32[8,768]{1,0:T(8,128)}, f32[8,768]{1,0:T(8,128)}, u32[]{:S(2)}, u32[]{:S(2)}) collective-permute-start(f32[8,768]{1,0:T(8,128)} %get-tuple-element.73), channel_id=1, source_target_pairs={{0,27},{1,28},{2,29},{3,30},{4,31},{5,32},{6,33},{7,34},{8,35},{9,... | collective-permute-start | bytes 73736
  999.9 21.1 %collective-permute-start.57 = (f32[8,768]{1,0:T(8,128)}, f32[8,768]{1,0:T(8,128)}, u32[]{:S(2)}, u32[]{:S(2)}) collective-permute-start(f32[8,768]{1,0:T(8,128)} %get-tuple-element.73), channel_id=1, source_target_pairs={{0,26},{1,27},{2,28},{3,29},{4,30},{5,31},{6,32},{7,33},{8,34},{9,... | collective-permute-start | bytes 73736
  1001.8 21.1 %collective-permute-start.56 = (f32[8,768]{1,0:T(8,128)}, f32[8,768]{1,0:T(8,128)}, u32[]{:S(2)}, u32[]{:S(2)}) collective-permute-start(f32[8,768]{1,0:T(8,128)} %get-tuple-element.73), channel_id=1, source_target_pairs={{0,25},{1,26},{2,27},{3,28},{4,29},{5,30},{6,31},{7,32},{8,33},{9,... | collective-permute-start | bytes 73736
  1003.7 21.5 %collective-permute-start.55 = (f32[8,768]{1,0:T(8,128)}, f32[8,768]{1,0:T(8,128)}, u32[]{:S(2)}, u32[]{:S(2)}) collective-permute-start(f32[8,768]{1,0:T(8,128)} %get-tuple-element.73), channel_id=1, source_target_pairs={{0,24},{1,25},{2,26},{3,27},{4,28},{5,29},{6,30},{7,31},{8,32},{9,... | collective-permute-start | bytes 73736
  1005.6 22.8 %collective-permute-start.54 = (f32[8,768]{1,0:T(8,128)}, f32[8,768]{1,0:T(8,128)}, u32[]{:S(2)}, u32[]{:S(2)}) collective-permute-start(f32[8,768]{1,0:T(8,128)} %get-tuple-element.73), channel_id=1, source_target_pairs={{0,23},{1,24},{2,25},{3,26},{4,27},{5,28},{6,29},{7,30},{8,31},{9,... | collective-permute-start | bytes 73736
  1051.6 17.0 %collective-permute-start.41 = (f32[8,768]{1,0:T(8,128)}, f32[8,768]{1,0:T(8,128)S(1)}, u32[]{:S(2)}, u32[]{:S(2)}) collective-permute-start(f32[8,768]{1,0:T(8,128)} %get-tuple-element.73), channel_id=1, source_target_pairs={{0,10},{1,11},{2,12},{3,13},{4,14},{5,15},{6,16},{7,17},{8,18},{9,... | collective-permute-start | bytes 73736
  1053.2 17.9 %collective-permute-start.40 = (f32[8,768]{1,0:T(8,128)}, f32[8,768]{1,0:T(8,128)S(1)}, u32[]{:S(2)}, u32[]{:S(2)}) collective-permute-start(f32[8,768]{1,0:T(8,128)} %get-tuple-element.73), channel_id=1, source_target_pairs={{0,9},{1,10},{2,11},{3,12},{4,13},{5,14},{6,15},{7,16},{8,17},{9,1... | collective-permute-start | bytes 73736
  1058.5 21.6 %collective-permute-start.39 = (f32[8,768]{1,0:T(8,128)}, f32[8,768]{1,0:T(8,128)}, u32[]{:S(2)}, u32[]{:S(2)}) collective-permute-start(f32[8,768]{1,0:T(8,128)} %get-tuple-element.73), channel_id=1, source_target_pairs={{0,8},{1,9},{2,10},{3,11},{4,12},{5,13},{6,14},{7,15},{8,16},{9,17... | collective-permute-start | bytes 73736
  1062.0 19.4 %collective-permute-start.38 = (f32[8,768]{1,0:T(8,128)}, f32[8,768]{1,0:T(8,128)}, u32[]{:S(2)}, u32[]{:S(2)}) collective-permute-start(f32[8,768]{1,0:T(8,128)} %get-tuple-element.73), channel_id=1, source_target_pairs={{0,7},{1,8},{2,9},{3,10},{4,11},{5,12},{6,13},{7,14},{8,15},{9,16}... | collective-permute-start | bytes 73736
  1068.6 17.1 %collective-permute-start.36 = (f32[8,768]{1,0:T(8,128)}, f32[8,768]{1,0:T(8,128)}, u32[]{:S(2)}, u32[]{:S(2)}) collective-permute-start(f32[8,768]{1,0:T(8,128)} %get-tuple-element.73), channel_id=1, source_target_pairs={{0,5},{1,6},{2,7},{3,8},{4,9},{5,10},{6,11},{7,12},{8,13},{9,14},{... | collective-permute-start | bytes 73736
  1128.2 78.8 %collective-permute-start.14 = (f32[8,2304]{1,0:T(8,128)}, f32[8,2304]{1,0:T(8,128)S(1)}, u32[]{:S(2)}, u32[]{:S(2)}) collective-permute-start(f32[8,2304]{1,0:T(8,128)} %get-tuple-element.72), channel_id=1, source_target_pairs={{0,15},{1,16},{2,17},{3,18},{4,19},{5,20},{6,21},{7,22},{8,23},{9,... | collective-permute-start | bytes 221192
  1129.6 79.4 %collective-permute-start.13 = (f32[8,2304]{1,0:T(8,128)}, f32[8,2304]{1,0:T(8,128)S(1)}, u32[]{:S(2)}, u32[]{:S(2)}) collective-permute-start(f32[8,2304]{1,0:T(8,128)} %get-tuple-element.72), channel_id=1, source_target_pairs={{0,14},{1,15},{2,16},{3,17},{4,18},{5,19},{6,20},{7,21},{8,22},{9,... | collective-permute-start | bytes 221192
  1130.9 81.3 %collective-permute-start.12 = (f32[8,2304]{1,0:T(8,128)}, f32[8,2304]{1,0:T(8,128)S(1)}, u32[]{:S(2)}, u32[]{:S(2)}) collective-permute-start(f32[8,2304]{1,0:T(8,128)} %get-tuple-element.72), channel_id=1, source_target_pairs={{0,13},{1,14},{2,15},{3,16},{4,17},{5,18},{6,19},{7,20},{8,21},{9,... | collective-permute-start | bytes 221192
  1132.2 82.6 %collective-permute-start.11 = (f32[8,2304]{1,0:T(8,128)}, f32[8,2304]{1,0:T(8,128)S(1)}, u32[]{:S(2)}, u32[]{:S(2)}) collective-permute-start(f32[8,2304]{1,0:T(8,128)} %get-tuple-element.72), channel_id=1, source_target_pairs={{0,12},{1,13},{2,14},{3,15},{4,16},{5,17},{6,18},{7,19},{8,20},{9,... | collective-permute-start | bytes 221192
  1138.7 81.7 %collective-permute-start.10 = (f32[8,2304]{1,0:T(8,128)}, f32[8,2304]{1,0:T(8,128)S(1)}, u32[]{:S(2)}, u32[]{:S(2)}) collective-permute-start(f32[8,2304]{1,0:T(8,128)} %get-tuple-element.72), channel_id=1, source_target_pairs={{0,11},{1,12},{2,13},{3,14},{4,15},{5,16},{6,17},{7,18},{8,19},{9,... | collective-permute-start | bytes 221192
  1207.1 46.1 %collective-permute-start.9 = (f32[8,2304]{1,0:T(8,128)}, f32[8,2304]{1,0:T(8,128)S(1)}, u32[]{:S(2)}, u32[]{:S(2)}) collective-permute-start(f32[8,2304]{1,0:T(8,128)} %get-tuple-element.72), channel_id=1, source_target_pairs={{0,10},{1,11},{2,12},{3,13},{4,14},{5,15},{6,16},{7,17},{8,18},{9,... | collective-permute-start | bytes 221192
  1209.0 45.6 %collective-permute-start.8 = (f32[8,2304]{1,0:T(8,128)}, f32[8,2304]{1,0:T(8,128)S(1)}, u32[]{:S(2)}, u32[]{:S(2)}) collective-permute-start(f32[8,2304]{1,0:T(8,128)} %get-tuple-element.72), channel_id=1, source_target_pairs={{0,9},{1,10},{2,11},{3,12},{4,13},{5,14},{6,15},{7,16},{8,17},{9,1... | collective-permute-start | bytes 221192
  1212.2 48.1 %collective-permute-start.7 = (f32[8,2304]{1,0:T(8,128)}, f32[8,2304]{1,0:T(8,128)S(1)}, u32[]{:S(2)}, u32[]{:S(2)}) collective-permute-start(f32[8,2304]{1,0:T(8,128)} %get-tuple-element.72), channel_id=1, source_target_pairs={{0,8},{1,9},{2,10},{3,11},{4,12},{5,13},{6,14},{7,15},{8,16},{9,17... | collective-permute-start | bytes 221192
  1214.9 46.7 %collective-permute-start.6 = (f32[8,2304]{1,0:T(8,128)}, f32[8,2304]{1,0:T(8,128)S(1)}, u32[]{:S(2)}, u32[]{:S(2)}) collective-permute-start(f32[8,2304]{1,0:T(8,128)} %get-tuple-element.72), channel_id=1, source_target_pairs={{0,7},{1,8},{2,9},{3,10},{4,11},{5,12},{6,13},{7,14},{8,15},{9,16}... | collective-permute-start | bytes 221192
  1220.4 44.9 %collective-permute-start.5 = (f32[8,2304]{1,0:T(8,128)}, f32[8,2304]{1,0:T(8,128)S(1)}, u32[]{:S(2)}, u32[]{:S(2)}) collective-permute-start(f32[8,2304]{1,0:T(8,128)} %get-tuple-element.72), channel_id=1, source_target_pairs={{0,6},{1,7},{2,8},{3,9},{4,10},{5,11},{6,12},{7,13},{8,14},{9,15},... | collective-permute-start | bytes 221192
  (206 other events, 4192.7 us)
Sparse Core Ops, SparseCore 0:
  10.8 66.6 all-gather.13
  80.6 64.6 all-gather.11
  146.9 101.4 all-gather.7
  249.9 91.8 all-gather.9
  522.5 18.2 reduce-scatter.28
  543.2 20.6 reduce-scatter.24
  566.3 20.5 reduce-scatter.22
  589.9 20.6 reduce-scatter.26
  615.4 144.3 all-reduce.15
  762.1 86.6 reduce-scatter.20
  851.3 106.5 reduce-scatter.18
where the time goes:
time: 1330 us; the launch traced here: 1310 us
  blocking collectives  595 us (45%)
  starting transfers between devices  206 us (15%)
  waiting for transfers between devices  195 us (15%)
  matrix products  139 us (10%)
  local copies, waits for them, and re-layouts  124 us (9%)
  other arithmetic  31.3 us (2%)
  between operations  17.4 us (1%)
    unnamed x3, blocking collectives  504 us
    unnamed x69, starting transfers between devices  168 us
    all_gather x1, waiting for transfers between devices, body(): lax.all_gather(w_out, 'dp', axis=1, tiled=True)  86.6 us
    unnamed x337, local copies, waits for them, and re-layouts  82.1 us
    all_gather x1, blocking collectives, body(): lax.all_gather(wr, ('dp', 'expert'), axis=0, tiled=True)  33.3 us
    unnamed x80, waiting for transfers between devices  30 us
    all_gather x2, blocking collectives, body(): lax.all_gather(qkv[:, width:2 * width], 'dp', axis=0, tiled=True)  29.5 us
    all_gather x2, blocking collectives, body(): lax.all_gather(qkv[:, 2 * width:], 'dp', axis=0, tiled=True)  28.4 us
  transfers between devices with their start and end apart: 83, of which 12 were waited for; matrix products, arithmetic and copies ran while one was open for 44% of the time, Pallas kernels for 0%

commit v1 on v0

v1 whole, which is shorter than its diff:
```python
import math

import jax
import jax.numpy as jnp
from jax import lax
from jax.sharding import Mesh
from jax.sharding import PartitionSpec as P

HEADS = 12
HEAD_DIM = 64
BUCKETS = 32
CAP = 3
FAR_STEP = 6
WIDTH = 768
TOK = 64
MB = 2
NY = 4
NEX = 32
HG = HEADS // NY
EX = ("z", "x", "c")
F32 = jnp.float32
BF = jnp.bfloat16

UP = [(i, (i + 1) % NY) for i in range(NY)]
DOWN = [(i, (i - 1) % NY) for i in range(NY)]
ACROSS = [(i, (i + 2) % NY) for i in range(NY)]


def mm(a, b):
    return lax.dot_general(a, b, (((1,), (0,)), ((), ())), preferred_element_type=F32)


def mm_nt(a, b):
    return lax.dot_general(a, b, (((1,), (1,)), ((), ())), preferred_element_type=F32)


def mm_tn(a, b):
    return lax.dot_general(a, b, (((0,), (0,)), ((), ())), preferred_element_type=F32)


def gather_y(piece):
    below = lax.ppermute(piece, "y", UP)
    above = lax.ppermute(piece, "y", DOWN)
    half = piece.shape[0] // 2
    first = lax.ppermute(below[:half], "y", UP)
    second = lax.ppermute(above[half:], "y", DOWN)
    return piece, below, above, jnp.concatenate([first, second], axis=0)


def scatter_y(own, below, above, across):
    half = own.shape[0] // 2
    first = lax.ppermute(across[:half], "y", UP)
    second = lax.ppermute(across[half:], "y", DOWN)
    up = jnp.concatenate(
        [(above[:half].astype(F32) + first.astype(F32)).astype(BF), above[half:]], axis=0
    )
    down = jnp.concatenate(
        [below[:half], (below[half:].astype(F32) + second.astype(F32)).astype(BF)], axis=0
    )
    from_below = lax.ppermute(up, "y", UP)
    from_above = lax.ppermute(down, "y", DOWN)
    return own.astype(F32) + from_below.astype(F32) + from_above.astype(F32)


def gather_four(piece, axis):
    return [piece] + [lax.ppermute(piece, axis, way) for way in (UP, DOWN, ACROSS)]


def owner_at(step, axis):
    shift = jnp.where(step == 1, 3, jnp.where(step == 2, 1, jnp.where(step == 3, 2, 0)))
    return (lax.axis_index(axis) + shift) % 4


def natural(pieces, place):
    stacked = jnp.stack([pieces[0], pieces[2], pieces[3], pieces[1]])
    return jnp.roll(stacked, place, axis=0)


def relative(stacked, place):
    return tuple(
        lax.dynamic_index_in_dim(stacked, (place + step) % NY, 0, keepdims=False)
        for step in (0, 3, 1, 2)
    )


def rms_scale(values):
    return lax.rsqrt(jnp.mean(values * values, axis=-1, keepdims=True) + 1e-06)


def softmax_last(scores):
    peak = jnp.max(scores, axis=-1, keepdims=True)
    weights = jnp.exp(scores - peak)
    return weights / jnp.sum(weights, axis=-1, keepdims=True)


def body(
    inputs, wqkv, wo, wr, gain_one, gain_two, rel_bias, w_in, w_out, routes, lengths, cotangent
):
    place = lax.axis_index("y")
    span = TOK * NY
    tokens = MB * TOK
    x_own = inputs.reshape(tokens, WIDTH)
    dy_own = cotangent.reshape(tokens, WIDTH)
    cols = wqkv.reshape(6, 3, NY, 192).transpose(2, 0, 1, 3).reshape(NY, 6, 576)
    small = jnp.concatenate(
        [
            wr,
            gain_one[:, None],
            gain_two[:, None],
            jnp.pad(rel_bias, (0, 3))[:, None],
            jnp.zeros((6, 61), BF),
        ],
        axis=1,
    )
    to_y = jnp.concatenate([cols, jnp.broadcast_to(small[None], (NY, 6, 128))], axis=2)
    from_y = lax.all_to_all(to_y, "y", 0, 0).reshape(24, 704)
    pack = jnp.concatenate([from_y, wo.reshape(24, 192)], axis=1)
    packed = jnp.concatenate(gather_four(pack, "x"), axis=0)
    packed = jnp.concatenate(gather_four(packed, "z"), axis=0)
    packed = jnp.concatenate([packed, lax.ppermute(packed, "c", [(0, 1), (1, 0)])], axis=0)
    rows = jnp.arange(WIDTH, dtype=jnp.int32)
    step = rows // 24
    e_row = owner_at(step // 4 % 4, "z") * 8 + owner_at(step % 4, "x") * 2
    e_row = e_row + (lax.axis_index("c") + step // 16) % 2
    in_chunk = rows % 24
    natural_row = ((in_chunk // 6) * NEX + e_row) * 6 + in_chunk % 6
    perm = (rows[:, None] == natural_row[None, :]).astype(BF)
    weights = mm(perm, packed[:, :704]).astype(BF)
    w_heads = weights[:, :576]
    small_all = weights[:, 576:]
    full_router = small_all[:, :64]
    first_gain = small_all[:, 64].astype(F32)
    second_gain = small_all[:, 65].astype(F32)
    wo_row = e_row * 24 + in_chunk
    wo_perm = (rows[:, None] == wo_row[None, :]).astype(BF)
    wo_heads = mm(wo_perm, packed[:, 704:]).astype(BF).reshape(192, WIDTH)
    table = lax.dynamic_slice_in_dim(small_all[:, 66].reshape(NY, 32, 6), place, 1, 0)
    table = table[0, :, :3].reshape(HG, BUCKETS)
    shuffled = (rows // 6 % NEX) * 24 + (rows // (6 * NEX)) * 6 + rows % 6
    grad_perm = (shuffled[:, None] == rows[None, :]).astype(BF)
    route = routes.reshape(MB, 2 * TOK)
    flat = jnp.arange(2 * TOK, dtype=jnp.int32)
    same = (route[:, :, None] == route[:, None, :]) & (flat[:, None] > flat[None, :])[None]
    slot = jnp.sum(same.astype(jnp.int32), axis=2)
    slot = jnp.arange(MB, dtype=jnp.int32)[:, None] * CAP + slot
    slot = slot.reshape(tokens, 2)
    both = route.reshape(tokens, 2)
    side = both % 2
    dest = (both // 2) * 8
    buffer_rows = jnp.arange(256, dtype=jnp.int32)
    pick, spare, spare_low = [], [], []
    for n in range(2):
        here = [side[:, k : k + 1] == n for k in range(2)]
        for kept, at in ((pick, dest + slot), (spare, dest + 6), (spare_low, dest + 7)):
            kept.append(
                [
                    ((buffer_rows[None, :] == at[:, k : k + 1]) & here[k]).astype(BF)
                    for k in range(2)
                ]
            )
    lanes = jnp.arange(WIDTH, dtype=jnp.int32)
    lane_mark = [(lanes[None, :] == slot[:, k : k + 1]) for k in range(2)]
    slots = jnp.arange(192, dtype=jnp.int32)
    buffer_of = (slots // 6) * 8 + slots % 6
    compact = (buffer_of[:, None] == buffer_rows[None, :]).astype(BF)

    def to_experts(buffer):
        return lax.all_to_all(buffer.reshape(NEX, 8, WIDTH), EX, 0, 0).reshape(256, WIDTH)

    x_all = natural(gather_y(x_own), place).reshape(NY, MB, TOK, WIDTH)
    x_all = x_all.transpose(1, 0, 2, 3).reshape(MB * span, WIDTH).astype(F32)
    first_scale = rms_scale(x_all)
    normed = (x_all * first_scale * first_gain).astype(BF)
    qkv = mm(normed, w_heads).astype(BF)
    split = qkv.reshape(MB, span, 3, HG, HEAD_DIM)
    queries, keys, values = split[:, :, 0], split[:, :, 1], split[:, :, 2]
    places = jnp.arange(span, dtype=jnp.int32)
    gap = jnp.maximum(places[:, None] - places[None, :], 0)
    bucket = jnp.where(gap < 16, gap, jnp.minimum(BUCKETS - 1, 16 + (gap - 16) // FAR_STEP))
    marks = (
        bucket.reshape(1, span * span) == jnp.arange(BUCKETS, dtype=jnp.int32)[:, None]
    ).astype(BF)
    bias = mm(table, marks).reshape(1, HG, span, span)
    bounds = jnp.cumsum(lengths.reshape(MB, 3), axis=1)[:, :2]
    segment = jnp.sum((places[None, :, None] >= bounds[:, None, :]).astype(jnp.int32), axis=2)
    allowed = (segment[:, :, None] == segment[:, None, :]) & (
        places[:, None] >= places[None, :]
    )[None]
    scale = 1.0 / math.sqrt(HEAD_DIM)
    raw = jnp.einsum("mqhd,mkhd->mhqk", queries, keys, preferred_element_type=F32)
    scores = jnp.where(allowed[:, None], raw * scale + bias, -1000000000.0)
    probs = softmax_last(scores)
    probs_low = probs.astype(BF)
    mixed = jnp.einsum("mhqk,mkhd->mqhd", probs_low, values, preferred_element_type=F32)
    mixed = mixed.reshape(MB * span, 192).astype(BF)
    branch = mm(mixed, wo_heads).astype(BF)
    dy_later, branch = lax.optimization_barrier((dy_own, branch))
    dy_rows = []
    for n in range(2):
        sent = mm_tn(pick[n][0] + pick[n][1], dy_later).astype(BF)
        dy_rows.append(
            jnp.concatenate(gather_y(mm(compact, to_experts(sent)).astype(BF)), axis=0)
        )

    def by_owner(rows_all):
        ordered = rows_all.reshape(MB, NY, TOK, WIDTH).transpose(1, 0, 2, 3)
        return relative(ordered.reshape(NY, tokens, WIDTH), place)

    x = x_own.astype(F32)
    middle = x + scatter_y(*by_owner(branch))
    second_scale = rms_scale(middle)
    entering = (middle * second_scale * second_gain).astype(BF)
    logits = mm(entering, full_router)
    expert_ids = jnp.arange(64, dtype=jnp.int32)
    routed = [
        (route.reshape(tokens, 2)[:, k : k + 1] == expert_ids[None, :]).astype(F32)
        for k in range(2)
    ]
    chosen = jnp.stack([jnp.sum(mark * logits, axis=1) for mark in routed], axis=1)
    gates = softmax_last(chosen)
    gates_high = gates.astype(BF).astype(F32)
    gates_low = gates - gates_high
    arrived = []
    for n in range(2):
        buffer = mm_tn(pick[n][0] + pick[n][1], entering)
        for k in range(2):
            mark = lane_mark[k].astype(F32)
            high = (mark * gates_high[:, k : k + 1]).astype(BF)
            low = (mark * gates_low[:, k : k + 1]).astype(BF)
            buffer = buffer + mm_tn(spare[n][k], high) + mm_tn(spare_low[n][k], low)
        arrived.append(to_experts(buffer.astype(BF)))
    w_in_of = [w_in[n] for n in range(2)]
    w_out_of = [w_out[n] for n in range(2)]
    rows_all, actives, pulled_of, slopes, d_backs = [], [], [], [], []
    back_lane = (slots % 6)[:, None] == lanes[None, :]
    back_spare = ((slots // 6 * 8 + 6)[:, None] == buffer_rows[None, :]).astype(BF)
    back_spare_low = ((slots // 6 * 8 + 7)[:, None] == buffer_rows[None, :]).astype(BF)

    def home(rows_of):
        return scatter_y(*[rows_of[192 * n : 192 * n + 192] for n in range(4)])

    for n in range(2):
        rows_n = jnp.concatenate(gather_y(mm(compact, arrived[n]).astype(BF)), axis=0)
        pulled = mm_nt(dy_rows[n], w_out_of[n])
        raised = mm(rows_n, w_in_of[n])
        gelu_value, gelu_pull = jax.vjp(jax.nn.gelu, raised)
        active = gelu_value.astype(BF)
        slope = gelu_pull(jnp.ones_like(raised))[0]
        d_raised = slope * pulled
        d_arrived = mm_nt(d_raised.astype(BF), w_in_of[n]).astype(BF)
        d_gate = jnp.sum(active.astype(F32) * pulled, axis=1)
        d_gate_rows = d_gate[:192]
        for i, way in ((1, DOWN), (2, UP), (3, ACROSS)):
            d_gate_rows = d_gate_rows + lax.ppermute(
                d_gate[192 * i : 192 * i + 192], "y", way
            )
        d_gate_rows = d_gate_rows.reshape(192, 1)
        d_gate_high = d_gate_rows.astype(BF).astype(F32)
        d_gate_low = d_gate_rows - d_gate_high
        back = mm_tn(compact, home(d_arrived).astype(BF))
        back = back + mm_tn(back_spare, jnp.where(back_lane, d_gate_high, 0.0).astype(BF))
        back = back + mm_tn(back_spare_low, jnp.where(back_lane, d_gate_low, 0.0).astype(BF))
        d_backs.append(to_experts(back.astype(BF)))
        rows_all.append(rows_n)
        actives.append(active)
        slopes.append(d_raised)
    grads_in, grads_out, returned = [], [], []
    for n in range(2):
        gate_rows = arrived[n].reshape(NEX, 8, WIDTH)[:, 6:8, :6].astype(F32).sum(axis=1)
        gate_all = jnp.concatenate(gather_four(gate_rows.reshape(192), "y"), axis=0)[:, None]
        active_late, d_back_late = lax.optimization_barrier((actives[n], d_backs[1]))
        d_backs[1] = d_back_late
        result = mm(active_late, w_out_of[n]).astype(BF)
        returned.append(to_experts(mm_tn(compact, home(result).astype(BF)).astype(BF)))
        grads_in.append(mm_tn(rows_all[n], (slopes[n] * gate_all).astype(BF)))
        d_returned = (dy_rows[n].astype(F32) * gate_all).astype(BF)
        grads_out.append(mm_tn(actives[n], d_returned))
    grad_in = jnp.stack(grads_in)
    grad_out = jnp.stack(grads_out)
    mixture = sum(
        gates[:, k : k + 1] * (mm(pick[0][k], returned[0]) + mm(pick[1][k], returned[1]))
        for k in range(2)
    )
    output = (middle + mixture).astype(BF)
    d_gates = jnp.stack(
        [
            jnp.sum(
                jnp.where(
                    lane_mark[k],
                    sum(mm(spare[n][k] + spare_low[n][k], d_backs[n]) for n in range(2)),
                    0.0,
                ),
                axis=1,
            )
            for k in range(2)
        ],
        axis=1,
    )
    d_chosen = gates * (d_gates - jnp.sum(gates * d_gates, axis=1, keepdims=True))
    d_logits = sum(d_chosen[:, k : k + 1] * routed[k] for k in range(2)).astype(BF)
    d_entering = sum(
        gates[:, k : k + 1] * (mm(pick[0][k], d_backs[0]) + mm(pick[1][k], d_backs[1]))
        for k in range(2)
    )
    d_entering = d_entering + mm_nt(d_logits, full_router)
    grad_wr = mm_tn(entering, d_logits)
    grad_gain_two = jnp.sum(d_entering * middle * second_scale, axis=0)
    scaled = d_entering * second_gain
    inner = jnp.mean(scaled * middle, axis=1, keepdims=True)
    dy = dy_own.astype(F32)
    d_middle = dy + second_scale * scaled - middle * second_scale**3 * inner
    d_branch = natural(gather_y(d_middle.astype(BF)), place).reshape(NY, MB, TOK, WIDTH)
    d_branch = d_branch.transpose(1, 0, 2, 3).reshape(MB * span, WIDTH)
    grad_wo = mm_tn(mixed, d_branch)
    d_mixed = mm_nt(d_branch, wo_heads).astype(BF).reshape(MB, span, HG, HEAD_DIM)
    d_probs = jnp.einsum("mqhd,mkhd->mhqk", d_mixed, values, preferred_element_type=F32)
    d_values = jnp.einsum("mhqk,mqhd->mkhd", probs_low, d_mixed, preferred_element_type=F32)
    d_scores = probs * (d_probs - jnp.sum(probs * d_probs, axis=-1, keepdims=True))
    d_sum = jnp.sum(d_scores, axis=0).reshape(HG, span * span)
    d_sum_high = d_sum.astype(BF)
    d_sum_low = (d_sum - d_sum_high.astype(F32)).astype(BF)
    grad_table = mm_nt(d_sum_high, marks) + mm_nt(d_sum_low, marks)
    d_raw = (d_scores * scale).astype(BF)
    d_queries = jnp.einsum("mhqk,mkhd->mqhd", d_raw, keys, preferred_element_type=F32)
    d_keys = jnp.einsum("mhqk,mqhd->mkhd", d_raw, queries, preferred_element_type=F32)
    d_qkv = jnp.stack([d_queries, d_keys, d_values], axis=2).reshape(MB * span, 576).astype(BF)
    grad_heads = mm_tn(normed, d_qkv)
    d_normed = mm_nt(d_qkv, w_heads)
    grad_gain_one = jnp.sum(d_normed * x_all * first_scale, axis=0)
    d_normed_own = scatter_y(*by_owner(d_normed.astype(BF)))
    scale_own = rms_scale(x)
    scaled_one = d_normed_own * first_gain
    inner_one = jnp.mean(scaled_one * x, axis=1, keepdims=True)
    input_grad = d_middle + scale_own * scaled_one - x * scale_own**3 * inner_one
    table_column = jnp.pad(grad_table.reshape(1, 32, 3), ((0, 0), (0, 0), (0, 3)))
    table_column = (
        jnp.where((jnp.arange(NY) == place)[:, None, None], table_column, 0.0)
    ).reshape(WIDTH, 1)
    grad_small = jnp.concatenate(
        [
            grad_wr,
            grad_gain_one[:, None],
            grad_gain_two[:, None],
            table_column,
            jnp.zeros((WIDTH, 61), F32),
        ],
        axis=1,
    )
    grad_pack = mm_tn(grad_perm, jnp.concatenate([grad_heads, grad_small], axis=1).astype(BF))
    grad_pack = jnp.concatenate(
        [grad_pack.astype(BF), grad_wo.astype(BF).reshape(WIDTH, 192)], axis=1
    )
    terms = lax.all_to_all(grad_pack.reshape(NEX, 24, 896), EX, 0, 0)
    summed = jnp.sum(terms.astype(F32), axis=0)
    wo_out = summed[:, 704:].reshape(6, WIDTH)
    mine = lax.all_to_all(summed[:, :704].reshape(NY, 6, 704), "y", 0, 0)
    wqkv_out = mine[:, :, :576].reshape(NY, 6, 3, 192).transpose(1, 2, 0, 3).reshape(6, 2304)
    small_out = jnp.sum(mine[:, :, 576:], axis=0)
    return (
        output.reshape(MB, 1, TOK, WIDTH),
        input_grad.reshape(MB, 1, TOK, WIDTH),
        wqkv_out,
        wo_out,
        small_out[:, :64],
        small_out[:, 64],
        small_out[:, 65],
        small_out[:3, 66],
        grad_in,
        grad_out,
    )


def solution(mesh):
    grid = Mesh(mesh.devices.reshape(NY, 4, 4, 2), ("y", "z", "x", "c"))
    every = ("y",) + EX
    in_specs = (
        P(None, EX, "y", None),
        P(every, None),
        P(every, None),
        P(every, None),
        P(every),
        P(every),
        P(every),
        P(EX, None, "y"),
        P(EX, "y", None),
        P(None, EX, "y", None),
        P(None, EX, None),
        P(None, EX, "y", None),
    )
    out_specs = (
        P(None, EX, "y", None),
        P(None, EX, "y", None),
        P(every, None),
        P(every, None),
        P(every, None),
        P(every),
        P(every),
        P(every),
        P(EX, None, "y"),
        P(EX, "y", None),
    )
    return jax.shard_map(body, mesh=grid, in_specs=in_specs, out_specs=out_specs, check_vma=False)
```

time: 1330 us -> 462 us (0.35); the launches traced: 1310 us -> 455 us
  blocking collectives: 595 us -> 0 us
  waiting for transfers between devices: 195 us -> 90.2 us
  local copies, waits for them, and re-layouts: 124 us -> 65 us
  starting transfers between devices: 206 us -> 153 us
  matrix products: 139 us -> 96.8 us
  other arithmetic: 31.3 us -> 46.3 us
  between operations: 17.4 us -> 3.14 us
    unnamed x3 -> x0, blocking collectives: 504 us -> none
    unnamed x69 -> x0, starting transfers between devices: 168 us -> none
    all_gather x4 -> x0, waiting for transfers between devices: 112 us -> none  [the longest x1 86.6 us: body(): lax.all_gather(w_out, 'dp', axis=1, tiled=True)]
    ppermute x0 -> x67, starting transfers between devices: none -> 102 us  [the longest x12 20.9 us: gather_four(): lax.ppermute(piece, axis, way)]
    all_gather x5 -> x0, blocking collectives: 91.1 us -> none  [the longest x1 33.3 us: body(): lax.all_gather(wr, ('dp', 'expert'), axis=0, tiled=True)]
    unnamed x337 -> x216, local copies, waits for them, and re-layouts: 82.1 us -> 13.3 us
    dot_general x53 -> x68, matrix products: 139 us -> 93.5 us  [the longest x28 41.5 us: mm_tn(): lax.dot_general(a, b, (((0,), (0,)), ((), ())), preferred_element_type=F32)]
    ppermute x0 -> x67, waiting for transfers between devices: none -> 35.8 us  [the longest x6 10.5 us: gather_y(): second = lax.ppermute(above[half:], 'y', DOWN)]
  transfers between devices with their start and end apart: 83 -> 78, of which waited for: 12 -> 27; matrix products, arithmetic and copies ran while one was open for 44% -> 37% of each run, Pallas kernels for 0% -> 0%
where the time goes in v1:
time: 462 us; the launch traced here: 455 us
  starting transfers between devices  153 us (33%)
  matrix products  96.8 us (21%)
  waiting for transfers between devices  90.2 us (20%)
  local copies, waits for them, and re-layouts  65 us (14%)
  other arithmetic  46.3 us (10%)
    dot_general x28, matrix products, mm_tn(): lax.dot_general(a, b, (((0,), (0,)), ((), ())), preferred_element_type=F32)  41.5 us
    all_to_all x8, starting transfers between devices, to_experts(): lax.all_to_all(buffer.reshape(NEX, 8, WIDTH), EX, 0, 0).reshape(256, WIDTH)  38.1 us
    all_to_all x8, waiting for transfers between devices, to_experts(): lax.all_to_all(buffer.reshape(NEX, 8, WIDTH), EX, 0, 0).reshape(256, WIDTH)  32.9 us
    dot_general x26, matrix products, mm(): lax.dot_general(a, b, (((1,), (0,)), ((), ())), preferred_element_type=F32)  25.3 us
    ppermute x12, starting transfers between devices, gather_four(): lax.ppermute(piece, axis, way)  20.9 us
    ppermute x6, starting transfers between devices, gather_y(): above = lax.ppermute(piece, 'y', DOWN)  18.9 us
    all_to_all x1, waiting for transfers between devices, body(): terms = lax.all_to_all(grad_pack.reshape(NEX, 24, 896), EX, 0, 0)  17.4 us
    ppermute x6, starting transfers between devices, scatter_y(): from_above = lax.ppermute(down, 'y', DOWN)  17.3 us
  transfers between devices with their start and end apart: 78, of which 27 were waited for; matrix products, arithmetic and copies ran while one was open for 37% of the time, Pallas kernels for 0%

profile of v1, /device:TPU:0, one launch (start us, length us, event | category | flops | bytes accessed | tf_op | source)
XLA Modules:
  0.0 454.7 jit_solution(18282716055140015307)
XLA Ops:
  8.6 4.5 all-to-all-start
  35.6 3.9 collective-permute-start.9
  84.5 3.5 collective-permute-start.14
  89.2 4.6 %all-to-all-start.7 = ((bf16[32,8,768]{2,1,0:T(8,128)(2,1)}), bf16[32,8,768]{2,1,0:T(8,128)(2,1)}, u32[]{:S(2)}, u32[]{:S(2)}) async-start(bf16[32,8,768]{2,1,0:T(8,128)(2,1)} %fusion.53), calls=%async_computation.7 | async-start | bytes 786432 | tf_op jit(solution)/shard_map/all_to_all | solution.py:168
  104.1 5.9 %all-to-all-start.3 = ((bf16[32,8,768]{2,1,0:T(8,128)(2,1)}), bf16[32,8,768]{2,1,0:T(8,128)(2,1)S(1)}, u32[]{:S(2)}, u32[]{:S(2)}) async-start(bf16[32,8,768]{2,1,0:T(8,128)(2,1)} %fusion.50), calls=%async_computation.3 | async-start | bytes 786432 | tf_op jit(solution)/shard_map/all_to_all | solution.py:168
  114.3 6.0 %all-to-all-done.3 = bf16[32,8,768]{2,1,0:T(8,128)(2,1)S(1)} async-done(((bf16[32,8,768]{2,1,0:T(8,128)(2,1)}), bf16[32,8,768]{2,1,0:T(8,128)(2,1)S(1)}, u32[]{:S(2)}, u32[]{:S(2)}) %all-to-all-start.3) | async-done | bytes 393248 | tf_op jit(solution)/shard_map/all_to_all | solution.py:168
  120.3 3.9 all-to-all-start.2
  126.9 7.6 %all-to-all-done.2 = bf16[32,8,768]{2,1,0:T(8,128)(2,1)S(1)} async-done(((bf16[32,8,768]{2,1,0:T(8,128)(2,1)}), bf16[32,8,768]{2,1,0:T(8,128)(2,1)S(1)}, u32[]{:S(2)}, u32[]{:S(2)}) %all-to-all-start.2) | async-done | bytes 393248 | tf_op jit(solution)/shard_map/all_to_all | solution.py:168
  134.5 3.9 all-to-all-start.1
  152.5 3.7 collective-permute-start.65
  181.8 6.7 %collective-permute-done.45 = bf16[96,768]{0,1:T(8,128)(2,1)S(1)} collective-permute-done((bf16[96,768]{0,1:T(8,128)(2,1)S(1)}, bf16[96,768]{0,1:T(8,128)(2,1)S(1)}, u32[]{:S(2)}, u32[]{:S(2)}) %collective-permute-start.45) | collective-permute-done | bytes 147488 | tf_op jit(solution)/shard_map/ppermute | solution.py:46
  192.4 3.6 concatenate.106
  223.2 3.5 convolution_bitcast_fusion.3
  236.6 3.5 convolution_bitcast_fusion.2
  268.8 7.4 %all-to-all-start.4 = ((bf16[32,8,768]{2,1,0:T(8,128)(2,1)}), bf16[32,8,768]{2,1,0:T(8,128)(2,1)S(1)}, u32[]{:S(2)}, u32[]{:S(2)}) async-start(bf16[32,8,768]{2,1,0:T(8,128)(2,1)} %fusion.49), calls=%async_computation.4 | async-start | bytes 786432 | tf_op jit(solution)/shard_map/all_to_all | solution.py:168
  279.7 6.8 %all-to-all-done.4 = bf16[32,8,768]{2,1,0:T(8,128)(2,1)S(1)} async-done(((bf16[32,8,768]{2,1,0:T(8,128)(2,1)}), bf16[32,8,768]{2,1,0:T(8,128)(2,1)S(1)}, u32[]{:S(2)}, u32[]{:S(2)}) %all-to-all-start.4) | async-done | bytes 393248 | tf_op jit(solution)/shard_map/all_to_all | solution.py:168
  286.5 3.9 all-to-all-start.8
  290.4 5.0 %pad_maximum_fusion = f32[2,768,768]{2,1,0:T(8,128)} fusion(f32[1,768,768]{2,1,0:T(8,128)} %convolution_bitcast_fusion.2, f32[1,768,768]{2,1,0:T(8,128)} %convolution_bitcast_fusion.3), kind=kLoop, calls=%fused_computation.8 | loop fusion | flops 1179648 | bytes 9437184 | tf_op jit(solution)/shard_map/stack | solution.py:278
  330.4 3.5 collective-permute-start.56
  336.2 3.7 collective-permute-done.56
  345.7 3.7 convolution_bitcast_fusion.5
  349.4 4.2 convolution_bitcast_fusion.6
  353.6 4.4 fusion.422
  372.3 7.8 %concatenate.119 = bf16[768,704]{0,1:T(8,128)(2,1)} concatenate(bf16[768,576]{0,1:T(8,128)(2,1)} %convolution_convert_fusion.4, bf16[768,64]{0,1:T(8,128)(2,1)S(1)} %convolution_convert_fusion.18, bf16[768,1]{0,1:T(2,128)(2,1)S(1)} %broadcast_in_dim.101, bf16[768,1]{0,1:T(2,128)(2,1)S(1)} %copy-done.56, bf16[768,1]{0,1:T(2,128)(2,1)S(1)} %select_n.468, ...), dimensions={1} | concatenate | bytes 2162688 | tf_op jit(solution)/shard_map/concatenate | solution.py:349
  380.0 3.5 fusion.38
  386.1 4.6 %all-to-all-start.5 = ((bf16[32,8,768]{2,1,0:T(8,128)(2,1)}), bf16[32,8,768]{2,1,0:T(8,128)(2,1)S(1)}, u32[]{:S(2)}, u32[]{:S(2)}) async-start(bf16[32,8,768]{2,1,0:T(8,128)(2,1)} %fusion.51), calls=%async_computation.5 | async-start | bytes 786432 | tf_op jit(solution)/shard_map/all_to_all | solution.py:168
  401.1 4.0 all-to-all-start.6
  410.4 4.9 %all-to-all-done.6 = bf16[32,8,768]{2,1,0:T(8,128)(2,1)S(1)} async-done(((bf16[32,8,768]{2,1,0:T(8,128)(2,1)}), bf16[32,8,768]{2,1,0:T(8,128)(2,1)S(1)}, u32[]{:S(2)}, u32[]{:S(2)}) %all-to-all-start.6) | async-done | bytes 393248 | tf_op jit(solution)/shard_map/all_to_all | solution.py:168
  415.4 4.0 all-to-all-start.9
  423.6 17.4 %all-to-all-done.9 = bf16[32,24,896]{2,1,0:T(8,128)(2,1)S(1)} async-done(((bf16[32,24,896]{2,1,0:T(8,128)(2,1)}), bf16[32,24,896]{2,1,0:T(8,128)(2,1)S(1)}, u32[]{:S(2)}, u32[]{:S(2)}) %all-to-all-start.9) | async-done | bytes 1376288 | tf_op jit(solution)/shard_map/all_to_all | solution.py:353
  441.8 4.5 all-to-all-start.10
  448.0 4.1 all-to-all-done.10
  (586 shorter events, 289.6 us)
Async XLA Ops:
  0.7 42.8 %collective-permute-start = (bf16[128,768]{1,0:T(8,128)(2,1)}, bf16[128,768]{1,0:T(8,128)(2,1)S(1)}, u32[]{:S(2)}, u32[]{:S(2)}) collective-permute-start(bf16[128,768]{1,0:T(8,128)(2,1)} %bitcast.354), channel_id=1, source_target_pairs={{0,96},{32,0},{64,32},{96,64},{1,97},{33,1},{65,33},{97,65},{2,98}... | collective-permute-start | bytes 589832 | tf_op jit(solution)/shard_map/ppermute | solution.py:43
  3.8 42.9 %collective-permute-start.1 = (bf16[128,768]{1,0:T(8,128)(2,1)}, bf16[128,768]{1,0:T(8,128)(2,1)S(1)}, u32[]{:S(2)}, u32[]{:S(2)}) collective-permute-start(bf16[128,768]{1,0:T(8,128)(2,1)} %bitcast.355), channel_id=1, source_target_pairs={{0,32},{32,64},{64,96},{96,0},{1,33},{33,65},{65,97},{97,1},{2,34}... | collective-permute-start | bytes 589832 | tf_op jit(solution)/shard_map/ppermute | solution.py:42
  8.6 16.8 %all-to-all-start = ((bf16[4,6,704]{2,1,0:T(8,128)(2,1)}), bf16[4,6,704]{2,1,0:T(8,128)(2,1)S(1)}, u32[]{:S(2)}, u32[]{:S(2)}) async-start(bf16[4,6,704]{2,1,0:T(8,128)(2,1)} %copy.178), calls=%async_computation | async-start | bytes 98304 | tf_op jit(solution)/shard_map/all_to_all | solution.py:116
  89.2 14.9 %all-to-all-start.7 = ((bf16[32,8,768]{2,1,0:T(8,128)(2,1)}), bf16[32,8,768]{2,1,0:T(8,128)(2,1)}, u32[]{:S(2)}, u32[]{:S(2)}) async-start(bf16[32,8,768]{2,1,0:T(8,128)(2,1)} %fusion.53), calls=%async_computation.7 | async-start | bytes 786432 | tf_op jit(solution)/shard_map/all_to_all | solution.py:168
  104.1 16.2 %all-to-all-start.3 = ((bf16[32,8,768]{2,1,0:T(8,128)(2,1)}), bf16[32,8,768]{2,1,0:T(8,128)(2,1)S(1)}, u32[]{:S(2)}, u32[]{:S(2)}) async-start(bf16[32,8,768]{2,1,0:T(8,128)(2,1)} %fusion.50), calls=%async_computation.3 | async-start | bytes 786432 | tf_op jit(solution)/shard_map/all_to_all | solution.py:168
  134.5 16.5 %all-to-all-start.1 = ((bf16[32,8,768]{2,1,0:T(8,128)(2,1)}), bf16[32,8,768]{2,1,0:T(8,128)(2,1)S(1)}, u32[]{:S(2)}, u32[]{:S(2)}) async-start(bf16[32,8,768]{2,1,0:T(8,128)(2,1)} %fusion.55), calls=%async_computation.1 | async-start | bytes 786432 | tf_op jit(solution)/shard_map/all_to_all | solution.py:168
  144.1 16.0 %collective-permute-start.43 = (bf16[192,768]{0,1:T(8,128)(2,1)S(1)}, bf16[192,768]{0,1:T(8,128)(2,1)}, u32[]{:S(2)}, u32[]{:S(2)}) collective-permute-start(bf16[192,768]{0,1:T(8,128)(2,1)S(1)} %convolution_convert_fusion.7), channel_id=1, source_target_pairs={{0,96},{32,0},{64,32},{96,64},{1,97},{33,1},{65,33},{97,65},{2,98}... | collective-permute-start | bytes 884744 | tf_op jit(solution)/shard_map/ppermute | solution.py:43
  147.4 16.2 %collective-permute-start.42 = (bf16[192,768]{0,1:T(8,128)(2,1)S(1)}, bf16[192,768]{0,1:T(8,128)(2,1)}, u32[]{:S(2)}, u32[]{:S(2)}) collective-permute-start(bf16[192,768]{0,1:T(8,128)(2,1)S(1)} %convolution_convert_fusion.7), channel_id=1, source_target_pairs={{0,32},{32,64},{64,96},{96,0},{1,33},{33,65},{65,97},{97,1},{2,34}... | collective-permute-start | bytes 884744 | tf_op jit(solution)/shard_map/ppermute | solution.py:42
  149.5 14.8 %collective-permute-start.66 = (f32[192]{0:T(256)}, f32[192]{0:T(256)}, u32[]{:S(2)}, u32[]{:S(2)}) collective-permute-start(f32[192]{0:T(256)} %reshape.685), channel_id=1, source_target_pairs={{0,64},{32,96},{64,0},{96,32},{1,65},{33,97},{65,1},{97,33},{2,66}... | collective-permute-start | bytes 2312 | tf_op jit(solution)/shard_map/ppermute | solution.py:66
  170.3 29.0 %collective-permute-start.16 = (bf16[192,768]{1,0:T(8,128)(2,1)}, bf16[192,768]{1,0:T(8,128)(2,1)S(1)}, u32[]{:S(2)}, u32[]{:S(2)}) collective-permute-start(bf16[192,768]{1,0:T(8,128)(2,1)} %get-tuple-element.202), channel_id=1, source_target_pairs={{0,96},{32,0},{64,32},{96,64},{1,97},{33,1},{65,33},{97,65},{2,98}... | collective-permute-start | bytes 884744 | tf_op jit(solution)/shard_map/ppermute | solution.py:43
  173.1 28.9 %collective-permute-start.15 = (bf16[192,768]{1,0:T(8,128)(2,1)}, bf16[192,768]{1,0:T(8,128)(2,1)}, u32[]{:S(2)}, u32[]{:S(2)}) collective-permute-start(bf16[192,768]{1,0:T(8,128)(2,1)} %get-tuple-element.202), channel_id=1, source_target_pairs={{0,32},{32,64},{64,96},{96,0},{1,33},{33,65},{65,97},{97,1},{2,34}... | collective-permute-start | bytes 884744 | tf_op jit(solution)/shard_map/ppermute | solution.py:42
  173.1 29.8 %collective-permute-start.20 = (bf16[192,768]{1,0:T(8,128)(2,1)}, bf16[192,768]{1,0:T(8,128)(2,1)S(1)}, u32[]{:S(2)}, u32[]{:S(2)}) collective-permute-start(bf16[192,768]{1,0:T(8,128)(2,1)} %get-tuple-element.199), channel_id=1, source_target_pairs={{0,96},{32,0},{64,32},{96,64},{1,97},{33,1},{65,33},{97,65},{2,98}... | collective-permute-start | bytes 884744 | tf_op jit(solution)/shard_map/ppermute | solution.py:43
  176.3 29.9 %collective-permute-start.19 = (bf16[192,768]{1,0:T(8,128)(2,1)}, bf16[192,768]{1,0:T(8,128)(2,1)}, u32[]{:S(2)}, u32[]{:S(2)}) collective-permute-start(bf16[192,768]{1,0:T(8,128)(2,1)} %get-tuple-element.199), channel_id=1, source_target_pairs={{0,32},{32,64},{64,96},{96,0},{1,33},{33,65},{65,97},{97,1},{2,34}... | collective-permute-start | bytes 884744 | tf_op jit(solution)/shard_map/ppermute | solution.py:42
  199.4 15.6 %collective-permute-start.18 = (bf16[96,768]{1,0:T(8,128)(2,1)S(1)}, bf16[96,768]{1,0:T(8,128)(2,1)S(1)}, u32[]{:S(2)}, u32[]{:S(2)}) collective-permute-start(bf16[96,768]{1,0:T(8,128)(2,1)S(1)} %slice.528), channel_id=1, source_target_pairs={{0,96},{32,0},{64,32},{96,64},{1,97},{33,1},{65,33},{97,65},{2,98}... | collective-permute-start | bytes 442376 | tf_op jit(solution)/shard_map/ppermute | solution.py:46
  218.5 24.3 %collective-permute-start.50 = (f32[192]{0:T(256)S(1)}, f32[192]{0:T(256)S(1)}, u32[]{:S(2)}, u32[]{:S(2)}) collective-permute-start(f32[192]{0:T(256)S(1)} %get-tuple-element.164), channel_id=1, source_target_pairs={{0,96},{32,0},{64,32},{96,64},{1,97},{33,1},{65,33},{97,65},{2,98}... | collective-permute-start | bytes 2312 | tf_op jit(solution)/shard_map/ppermute | solution.py:254
  218.9 25.6 %collective-permute-start.52 = (f32[192]{0:T(256)S(1)}, f32[192]{0:T(256)S(1)}, u32[]{:S(2)}, u32[]{:S(2)}) collective-permute-start(f32[192]{0:T(256)S(1)} %get-tuple-element.165), channel_id=1, source_target_pairs={{0,64},{32,96},{64,0},{96,32},{1,65},{33,97},{65,1},{97,33},{2,66}... | collective-permute-start | bytes 2312 | tf_op jit(solution)/shard_map/ppermute | solution.py:254
  219.4 26.5 %collective-permute-start.51 = (f32[192]{0:T(256)S(1)}, f32[192]{0:T(256)S(1)}, u32[]{:S(2)}, u32[]{:S(2)}) collective-permute-start(f32[192]{0:T(256)S(1)} %get-tuple-element.166), channel_id=1, source_target_pairs={{0,32},{32,64},{64,96},{96,0},{1,33},{33,65},{65,97},{97,1},{2,34}... | collective-permute-start | bytes 2312 | tf_op jit(solution)/shard_map/ppermute | solution.py:254
  226.8 32.9 %collective-permute-start.46 = (bf16[96,768]{1,0:T(8,128)(2,1)S(1)}, bf16[96,768]{1,0:T(8,128)(2,1)S(1)}, u32[]{:S(2)}, u32[]{:S(2)}) collective-permute-start(bf16[96,768]{1,0:T(8,128)(2,1)S(1)} %get-tuple-element.115), channel_id=1, source_target_pairs={{0,32},{32,64},{64,96},{96,0},{1,33},{33,65},{65,97},{97,1},{2,34}... | collective-permute-start | bytes 442376 | tf_op jit(solution)/shard_map/ppermute | solution.py:52
  228.7 31.1 %collective-permute-start.48 = (bf16[96,768]{1,0:T(8,128)(2,1)S(1)}, bf16[96,768]{1,0:T(8,128)(2,1)S(1)}, u32[]{:S(2)}, u32[]{:S(2)}) collective-permute-start(bf16[96,768]{1,0:T(8,128)(2,1)S(1)} %get-tuple-element.116), channel_id=1, source_target_pairs={{0,96},{32,0},{64,32},{96,64},{1,97},{33,1},{65,33},{97,65},{2,98}... | collective-permute-start | bytes 442376 | tf_op jit(solution)/shard_map/ppermute | solution.py:53
  260.6 16.8 %collective-permute-start.49 = (bf16[192,768]{1,0:T(8,128)(2,1)}, bf16[192,768]{1,0:T(8,128)(2,1)}, u32[]{:S(2)}, u32[]{:S(2)}) collective-permute-start(bf16[192,768]{1,0:T(8,128)(2,1)} %pad_maximum_fusion.10), channel_id=1, source_target_pairs={{0,96},{32,0},{64,32},{96,64},{1,97},{33,1},{65,33},{97,65},{2,98}... | collective-permute-start | bytes 884744 | tf_op jit(solution)/shard_map/ppermute | solution.py:61
  268.8 17.7 %all-to-all-start.4 = ((bf16[32,8,768]{2,1,0:T(8,128)(2,1)}), bf16[32,8,768]{2,1,0:T(8,128)(2,1)S(1)}, u32[]{:S(2)}, u32[]{:S(2)}) async-start(bf16[32,8,768]{2,1,0:T(8,128)(2,1)} %fusion.49), calls=%async_computation.4 | async-start | bytes 786432 | tf_op jit(solution)/shard_map/all_to_all | solution.py:168
  308.4 21.9 %collective-permute-start.54 = (bf16[128,768]{1,0:T(8,128)(2,1)S(1)}, bf16[128,768]{1,0:T(8,128)(2,1)S(1)}, u32[]{:S(2)}, u32[]{:S(2)}) collective-permute-start(bf16[128,768]{1,0:T(8,128)(2,1)S(1)} %get-tuple-element.91), channel_id=1, source_target_pairs={{0,32},{32,64},{64,96},{96,0},{1,33},{33,65},{65,97},{97,1},{2,34}... | collective-permute-start | bytes 589832 | tf_op jit(solution)/shard_map/ppermute | solution.py:42
  308.4 22.0 %collective-permute-start.53 = (bf16[128,768]{1,0:T(8,128)(2,1)S(1)}, bf16[128,768]{1,0:T(8,128)(2,1)S(1)}, u32[]{:S(2)}, u32[]{:S(2)}) collective-permute-start(bf16[128,768]{1,0:T(8,128)(2,1)S(1)} %get-tuple-element.91), channel_id=1, source_target_pairs={{0,96},{32,0},{64,32},{96,64},{1,97},{33,1},{65,33},{97,65},{2,98}... | collective-permute-start | bytes 589832 | tf_op jit(solution)/shard_map/ppermute | solution.py:43
  322.3 61.5 %collective-permute-start.37 = (bf16[192,768]{1,0:T(8,128)(2,1)}, bf16[192,768]{1,0:T(8,128)(2,1)}, u32[]{:S(2)}, u32[]{:S(2)}) collective-permute-start(bf16[192,768]{1,0:T(8,128)(2,1)} %pad_maximum_fusion.6), channel_id=1, source_target_pairs={{0,96},{32,0},{64,32},{96,64},{1,97},{33,1},{65,33},{97,65},{2,98}... | collective-permute-start | bytes 884744 | tf_op jit(solution)/shard_map/ppermute | solution.py:61
  324.7 59.1 %collective-permute-start.35 = (bf16[192,768]{1,0:T(8,128)(2,1)}, bf16[192,768]{1,0:T(8,128)(2,1)}, u32[]{:S(2)}, u32[]{:S(2)}) collective-permute-start(bf16[192,768]{1,0:T(8,128)(2,1)} %pad_maximum_fusion.5), channel_id=1, source_target_pairs={{0,32},{32,64},{64,96},{96,0},{1,33},{33,65},{65,97},{97,1},{2,34}... | collective-permute-start | bytes 884744 | tf_op jit(solution)/shard_map/ppermute | solution.py:60
  327.7 67.7 %collective-permute-start.41 = (bf16[192,768]{1,0:T(8,128)(2,1)}, bf16[192,768]{1,0:T(8,128)(2,1)}, u32[]{:S(2)}, u32[]{:S(2)}) collective-permute-start(bf16[192,768]{1,0:T(8,128)(2,1)} %pad_maximum_fusion.8), channel_id=1, source_target_pairs={{0,96},{32,0},{64,32},{96,64},{1,97},{33,1},{65,33},{97,65},{2,98}... | collective-permute-start | bytes 884744 | tf_op jit(solution)/shard_map/ppermute | solution.py:61
  368.9 14.6 %collective-permute-start.57 = (bf16[64,768]{1,0:T(8,128)(2,1)S(1)}, bf16[64,768]{1,0:T(8,128)(2,1)S(1)}, u32[]{:S(2)}, u32[]{:S(2)}) collective-permute-start(bf16[64,768]{1,0:T(8,128)(2,1)S(1)} %get-tuple-element.139), channel_id=1, source_target_pairs={{0,32},{32,64},{64,96},{96,0},{1,33},{33,65},{65,97},{97,1},{2,34}... | collective-permute-start | bytes 294920 | tf_op jit(solution)/shard_map/ppermute | solution.py:52
  369.0 14.7 %collective-permute-start.59 = (bf16[64,768]{1,0:T(8,128)(2,1)S(1)}, bf16[64,768]{1,0:T(8,128)(2,1)S(1)}, u32[]{:S(2)}, u32[]{:S(2)}) collective-permute-start(bf16[64,768]{1,0:T(8,128)(2,1)S(1)} %get-tuple-element.141), channel_id=1, source_target_pairs={{0,96},{32,0},{64,32},{96,64},{1,97},{33,1},{65,33},{97,65},{2,98}... | collective-permute-start | bytes 294920 | tf_op jit(solution)/shard_map/ppermute | solution.py:53
  386.1 14.9 %all-to-all-start.5 = ((bf16[32,8,768]{2,1,0:T(8,128)(2,1)}), bf16[32,8,768]{2,1,0:T(8,128)(2,1)S(1)}, u32[]{:S(2)}, u32[]{:S(2)}) async-start(bf16[32,8,768]{2,1,0:T(8,128)(2,1)} %fusion.51), calls=%async_computation.5 | async-start | bytes 786432 | tf_op jit(solution)/shard_map/all_to_all | solution.py:168
  391.5 27.9 %collective-permute-start.60 = (bf16[128,768]{1,0:T(8,128)(2,1)}, bf16[128,768]{1,0:T(8,128)(2,1)}, u32[]{:S(2)}, u32[]{:S(2)}) collective-permute-start(bf16[128,768]{1,0:T(8,128)(2,1)} %pad_maximum_fusion.14), channel_id=1, source_target_pairs={{0,96},{32,0},{64,32},{96,64},{1,97},{33,1},{65,33},{97,65},{2,98}... | collective-permute-start | bytes 589832 | tf_op jit(solution)/shard_map/ppermute | solution.py:61
  395.4 24.0 %collective-permute-start.58 = (bf16[128,768]{1,0:T(8,128)(2,1)}, bf16[128,768]{1,0:T(8,128)(2,1)}, u32[]{:S(2)}, u32[]{:S(2)}) collective-permute-start(bf16[128,768]{1,0:T(8,128)(2,1)} %pad_maximum_fusion.13), channel_id=1, source_target_pairs={{0,32},{32,64},{64,96},{96,0},{1,33},{33,65},{65,97},{97,1},{2,34}... | collective-permute-start | bytes 589832 | tf_op jit(solution)/shard_map/ppermute | solution.py:60
  415.4 25.6 %all-to-all-start.9 = ((bf16[32,24,896]{2,1,0:T(8,128)(2,1)}), bf16[32,24,896]{2,1,0:T(8,128)(2,1)S(1)}, u32[]{:S(2)}, u32[]{:S(2)}) async-start(bf16[32,24,896]{2,1,0:T(8,128)(2,1)} %pad_maximum_fusion.2), calls=%async_computation.9 | async-start | bytes 2752512 | tf_op jit(solution)/shard_map/all_to_all | solution.py:353
  (145 other events, 1014.3 us)
